TPU v7x, 32 devices: a whole 2x2x4 slice. The times are simulated.
32 devices in a mesh: dp: 8 (over z, x), tensor: 4 (over y, core).
Axes of the slice: x: 2, y: 2, z: 4, core: 2. Of those that a mesh axis runs over, the one named last changes fastest.
Arguments:
- tokens: bfloat16 [9536, 768], P(('dp', 'tensor')), may hold values from -6 to 6
- lengths: int32 [8], P('dp'), may hold values from 397 to 1192, as said below
- ln1_gain: float32 [768], replicated, may hold values from 0.5 to 1.5
- ln1_shift: float32 [768], replicated, may hold values from -1.75 to 1.75
- qkv_weight: bfloat16 [768, 3, 768], P(None, None, 'tensor'), may hold values from -0.21875 to 0.21875
- qv_bias: float32 [2, 768], P(None, 'tensor'), may hold values from -1.75 to 1.75
- out_weight: bfloat16 [768, 768], P('tensor'), may hold values from -0.875 to 0.875
- out_bias: float32 [768], replicated, may hold values from -1.75 to 1.75
- ln2_gain: float32 [768], replicated, may hold values from 0.5 to 1.5
- ln2_shift: float32 [768], replicated, may hold values from -1.75 to 1.75
- up_weight: bfloat16 [768, 3072], P(None, 'tensor'), may hold values from -0.21875 to 0.21875
- up_bias: float32 [3072], P('tensor'), may hold values from -1.75 to 1.75
- down_weight: bfloat16 [3072, 768], P('tensor'), may hold values from -0.109375 to 0.109375
- down_bias: float32 [768], replicated, may hold values from -1.75 to 1.75
- cotangent: float32 [9536, 768], P(('dp', 'tensor')), may hold values from -6 to 6
Outputs:
- output: bfloat16 [9536, 768], P(('dp', 'tensor'))
- grad_tokens: float32 [9536, 768], P(('dp', 'tensor'))
- grad_ln1_gain: float32 [768], replicated
- grad_ln1_shift: float32 [768], replicated
- grad_qkv_weight: float32 [768, 3, 768], P(None, None, 'tensor')
- grad_qv_bias: float32 [2, 768], P(None, 'tensor')
- grad_out_weight: float32 [768, 768], P('tensor')
- grad_out_bias: float32 [768], replicated
- grad_ln2_gain: float32 [768], replicated
- grad_ln2_shift: float32 [768], replicated
- grad_up_weight: float32 [768, 3072], P(None, 'tensor')
- grad_up_bias: float32 [3072], P('tensor')
- grad_down_weight: float32 [3072, 768], P('tensor')
- grad_down_bias: float32 [768], replicated
Inputs may be any that keep to these rules, and one draw needn't show every extreme that they name: `lengths`: keys of a clip at positions from its length on are padding.
All inputs are finite; a program needn't handle non-finite values.
Results may differ from a plain program's by a relative error of at most 0.02.
Values may be sent and summed in bfloat16 or wider, within the bound.
A program may use at most 192 MiB of HBM per device.

v0:
```python
import types

import jax
import jax.numpy as jnp
from jax import lax
from jax.experimental import pallas as pl
from jax.experimental.pallas import tpu as pltpu
from jax.sharding import PartitionSpec as P

HEAD_DIM = 64
LOGICAL = pl.DeviceIdType.LOGICAL
VMEM_BYTES = 62 * 2**20

epsilon = 1e-06
low = jnp.bfloat16
wide = jnp.float32


def round_up(amount, unit):
    return -(-amount // unit) * unit


class Here:
    def __init__(self, dp, tensor):
        self.dp, self.tensor = dp, tensor
        self.d, self.t = lax.axis_index("dp"), lax.axis_index("tensor")
        self.me = self.d * tensor + self.t
        self.chip = lax.div(self.t, 2)
        self.core = self.t - 2 * self.chip
        self.bits, rest = [], self.d
        for _ in range(dp.bit_length() - 1):
            half = lax.div(rest, 2)
            self.bits.append(rest - 2 * half)
            rest = half
        low_bits = sum(bit * (1 << b) for b, bit in enumerate(self.bits[:3]))
        self.near, self.group = low_bits, self.d - low_bits

    def logical(self, dp=None, tensor=None):
        if dp is not None:
            return self.me + (dp - self.d) * self.tensor
        return self.me + (tensor - self.t)

    def bit_flipped(self, b):
        return self.d + (1 - 2 * self.bits[b]) * (1 << b)


def flipped(here, flip_chip, flip_core):
    chip = here.chip + flip_chip - 2 * here.chip * flip_chip
    return 2 * chip + here.core + flip_core - 2 * here.core * flip_core


def two_bits(i):
    high = jnp.where(i >= 2, 1, 0)
    return high, i - 2 * high


def dot(left, right):
    return jnp.dot(left, right, preferred_element_type=wide)


def dot_rows(left, right):
    return lax.dot_general(left, right, (((1,), (1,)), ((), ())), preferred_element_type=wide)


def dot_columns(left, right):
    return lax.dot_general(left, right, (((0,), (0,)), ((), ())), preferred_element_type=wide)


def standardize(values):
    center = values - jnp.mean(values, -1, keepdims=True)
    inverse = lax.rsqrt(jnp.mean(center * center, -1, keepdims=True) + epsilon)
    return center * inverse, inverse


def norm_back(grad, unit, inverse, gain):
    scaled = grad * gain
    return inverse * (
        scaled
        - jnp.mean(scaled, -1, keepdims=True)
        - unit * jnp.mean(scaled * unit, -1, keepdims=True)
    )


def pair(ref, p):
    _, rows, columns = ref.shape
    return ref[pl.ds(2 * p, 2)].reshape(2 * rows, columns)


def set_pair(ref, p, values):
    ref[pl.ds(2 * p, 2)] = values.reshape(2, -1, values.shape[1])


def flat(ref):
    a, b, c = ref.shape
    return ref[...].reshape(a * b, c)


class Links:
    def __init__(self, here, send, recv):
        self.here, self.send, self.recv, self.used, self.pending = here, send, recv, 0, []

    def take(self, amount=1):
        base = self.used
        self.used += amount
        assert self.used <= self.send.shape[0]
        return base

    def copy(self, src, dst, at, **where):
        return pltpu.make_async_remote_copy(
            src_ref=src,
            dst_ref=dst,
            send_sem=self.send.at[at],
            recv_sem=self.recv.at[at],
            device_id=self.here.logical(**where),
            device_id_type=LOGICAL,
        )

    def start(self, src, dst, at, **where):
        copy = self.copy(src, dst, at, **where)
        copy.start()
        self.pending.append(copy)

    def arrived(self, dst, at, **where):
        self.copy(dst, dst, at, **where).wait_recv()

    def finish(self):
        for copy in self.pending:
            copy.wait_send()
        self.pending = []


class Gather:
    def __init__(self, links, buf, here, parts):
        self.links, self.buf, self.t, self.parts = links, buf, here.t, parts
        self.cross, self.diag, self.sib = here.peers
        self.base = links.take(3 * len(parts))

    def view(self, slot, part):
        start, size = self.parts[part]
        return self.buf.at[slot, pl.ds(start, size)]

    def _each(self):
        return range(len(self.parts))

    def start(self, parts=None):
        parts = self._each() if parts is None else parts
        for p in parts:
            v = self.view(self.t, p)
            self.links.copy(v, v, self.base + 3 * p, tensor=self.cross).start()
        for p in parts:
            v = self.view(self.t, p)
            self.links.copy(v, v, self.base + 3 * p + 1, tensor=self.sib).start()

    def wait_sib(self):
        for p in self._each():
            self.links.arrived(self.view(self.sib, p), self.base + 3 * p + 1, tensor=self.sib)

    def forward(self, parts=None):
        for p in self._each() if parts is None else parts:
            v = self.view(self.cross, p)
            self.links.arrived(v, self.base + 3 * p, tensor=self.cross)
            self.links.copy(v, v, self.base + 3 * p + 2, tensor=self.sib).start()

    def wait_diag(self, parts=None):
        for p in self._each() if parts is None else parts:
            self.links.arrived(self.view(self.diag, p), self.base + 3 * p + 2, tensor=self.sib)

    def finish(self):
        for p in self._each():
            v = self.view(self.t, p)
            self.links.copy(v, v, self.base + 3 * p, tensor=self.cross).wait_send()
            self.links.copy(v, v, self.base + 3 * p + 1, tensor=self.sib).wait_send()
            v = self.view(self.cross, p)
            self.links.copy(v, v, self.base + 3 * p + 2, tensor=self.sib).wait_send()


class Reduce:
    def __init__(self, links, part, pre, near, far, here, parts):
        self.links, self.part, self.t, self.parts = links, part, here.t, parts
        self.pre, self.near, self.far = pre, near, far
        self.cross, self.diag, self.sib = here.peers
        self.base = links.take(3 * len(parts))

    def _copy(self, kind, p):
        slot, box, peer = (
            (self.diag, self.pre, self.sib),
            (self.sib, self.near, self.sib),
            (self.cross, self.far, self.cross),
        )[kind]
        rows = pl.ds(*self.parts[p])
        return self.links.copy(
            self.part.at[slot, rows], box.at[rows], self.base + 3 * p + kind, tensor=peer
        )

    def _each(self, parts):
        return range(len(self.parts)) if parts is None else parts

    def send_diag(self, parts=None):
        for p in self._each(parts):
            self._copy(0, p).start()

    def send_sib(self):
        for p in self._each(None):
            self._copy(1, p).start()

    def send_cross(self, parts=None):
        for p in self._each(parts):
            self._copy(0, p).wait_recv()
            rows = pl.ds(*self.parts[p])
            self.part[self.cross, rows] = (
                self.part[self.cross, rows].astype(wide) + self.pre[rows].astype(wide)
            ).astype(low)
            self._copy(2, p).start()

    def result(self, p):
        self._copy(1, p).wait_recv()
        self._copy(2, p).wait_recv()
        rows = pl.ds(*self.parts[p])
        return (
            self.part[self.t, rows].astype(wide)
            + self.near[rows].astype(wide)
            + self.far[rows].astype(wide)
        )

    def finish(self):
        for p in self._each(None):
            for kind in range(3):
                self._copy(kind, p).wait_send()


class DataReduce:
    def __init__(self, links, held, whole, out, box, box_at, first, rows):
        self.links, self.held, self.whole, self.out, self.here = links, held, whole, out, links.here
        count = self.here.dp
        bits = count.bit_length() - 1
        assert count == 1 << bits and bits >= 3
        self.extra = list(range(3, bits))
        self.region = (first, rows, 0, held.shape[1])
        self.trail, self.sent, self.boxes = [], [], []
        for tall, broad in self.sizes(rows, held.shape[1], count)[0]:
            self.boxes.append(box.at[pl.ds(box_at, tall), pl.ds(0, broad)])
            box_at += tall
        self.base = links.take(9 + len(self.extra))
        self.plan()

    @classmethod
    def sizes(cls, rows, columns, count):
        found = cls.boxes_of(rows, columns)
        found += found[-1:] * (count.bit_length() - 1 - 3)
        return found, sum(size[0] for size in found)

    def _bit(self, b):
        return self.here.bits[b]

    def _peer(self, b):
        return self.here.bit_flipped(b)

    def _send(self, src, dst, at, peer):
        copy = self.links.copy(src, dst, self.base + at, dp=peer)
        copy.start()
        self.sent.append(copy)

    def _wait(self, dst, at, peer):
        self.links.arrived(dst, self.base + at, dp=peer)

    @staticmethod
    def _view(ref, region):
        row, rows, column, columns = region
        if columns == ref.shape[1]:
            return ref.at[pl.ds(row, rows)]
        return ref.at[pl.ds(row, rows), pl.ds(column, columns)]

    @staticmethod
    def _part(region, bit):
        row, rows, column, columns = region
        if rows % 32 == 0:
            return (pl.multiple_of(row + bit * (rows // 2), 16), rows // 2, column, columns)
        return (row, rows, pl.multiple_of(column + bit * (columns // 2), 128), columns // 2)

    def _give_half(self, b, box, at):
        bit = self._bit(b)
        self.trail.append(self.region)
        self._send(self._view(self.held, self._part(self.region, 1 - bit)), self.boxes[box], at, self._peer(b))
        self.region = self._part(self.region, bit)

    def _add(self, boxes, last):
        view = self._view(self.held, self.region)
        total = view[...].astype(wide)
        for box in boxes:
            total += self.boxes[box][...].astype(wide)
        if last:
            view = self._view(self.whole, self.region)
        view[...] = total.astype(low)
        if last:
            self._swap()

    def _swap(self):
        view = self._view(self.whole, self.region)
        for k, b in enumerate(self.extra):
            box, at = self.boxes[k - len(self.extra)], 9 + k
            copy = self.links.copy(view, box, self.base + at, dp=self._peer(b))
            copy.start()
            self._wait(box, at, self._peer(b))
            copy.wait_send()
            view[...] = (view[...].astype(wide) + box[...].astype(wide)).astype(low)

    def _give_whole(self, b, at):
        view = self._view(self.whole, self.region)
        self._send(view, view, at, self._peer(b))

    def _take_half(self, b, at):
        outer = self.trail.pop()
        view = self._view(self.whole, self._part(outer, 1 - self._bit(b)))
        self._wait(view, at, self._peer(b))
        self.region = outer

    def _leave(self):
        rows = pl.ds(self.region[0], self.region[1])
        self.left = pltpu.make_async_copy(
            self.whole.at[rows], self.out.at[rows], self.links.send.at[self.base + 8]
        )
        self.left.start()

    def step(self):
        if self.steps:
            self.steps.pop(0)()

    def finish(self):
        assert not self.steps
        self.left.wait()
        for copy in self.sent:
            copy.wait_send()


class Halves(DataReduce):
    order = (1, 0, 2)

    @staticmethod
    def boxes_of(rows, columns):
        found = []
        for _ in range(3):
            if rows % 32 == 0:
                rows //= 2
            else:
                columns //= 2
            found.append((rows, columns))
        return found

    def plan(self):
        a, b, c = self.order
        self.steps = [
            lambda: self._give_half(a, 0, 0),
            lambda: (self._wait_box(a, 0), self._add((0,), False), self._give_half(b, 1, 1)),
            lambda: (self._wait_box(b, 1), self._add((1,), False), self._give_half(c, 2, 2)),
            lambda: (self._wait_box(c, 2), self._add((2,), True), self._give_whole(c, 3)),
            lambda: (self._take_half(c, 3), self._give_whole(b, 4)),
            lambda: (self._take_half(b, 4), self._give_whole(a, 5)),
            lambda: (self._take_half(a, 5), self._leave()),
        ]

    def _wait_box(self, b, box):
        self._wait(self.boxes[box], box, self._peer(b))


class HalvesFromX(Halves):
    order = (0, 1, 2)


class Quarters(DataReduce):
    @staticmethod
    def boxes_of(rows, columns):
        tall, broad = rows // 8, columns
        if tall % 16:
            tall, broad = rows // 4, columns // 2
        return [(rows // 2, columns)] + [(tall, broad)] * 3

    def plan(self):
        self.steps = [
            lambda: self._give_half(0, 0, 0),
            lambda: (self._wait(self.boxes[0], 0, self._peer(0)), self._add((0,), False), self._give_quarters()),
            lambda: (self._take_boxes(), self._add((1, 2, 3), True), self._give_quarter()),
            lambda: (self._take_quarters(), self._give_whole(0, 7)),
            lambda: (self._take_half(0, 7), self._leave()),
        ]

    def _z(self, j):
        low_bit = 1 - self._bit(1) if j % 2 else self._bit(1)
        high = 1 - self._bit(2) if j // 2 else self._bit(2)
        return low_bit, high, self.here.group + high * 4 + low_bit * 2 + self._bit(0)

    def _quarter(self, j):
        low_bit, high, peer = self._z(j)
        return self._part(self._part(self.trail[-1], high), low_bit), peer

    def _give_quarters(self):
        self.trail.append(self.region)
        for j in (1, 2, 3):
            part, peer = self._quarter(j)
            self._send(self._view(self.held, part), self.boxes[j], j, peer)
        self.region = self._quarter(0)[0]

    def _take_boxes(self):
        for j in (1, 2, 3):
            self._wait(self.boxes[j], j, self._z(j)[2])

    def _give_quarter(self):
        view = self._view(self.whole, self.region)
        for j in (1, 2, 3):
            self._send(view, view, 3 + j, self._z(j)[2])

    def _take_quarters(self):
        for j in (1, 2, 3):
            part, peer = self._quarter(j)
            self._wait(self._view(self.whole, part), 3 + j, peer)
        self.region = self.trail.pop()


class Pipeline:
    def __init__(self, plan):
        self.plan, self.members = plan, []

    def add(self, member):
        self.members.append(member)
        member.step()

    def at(self, place):
        for number in self.plan[place]:
            self.members[number].step()

    def finish(self):
        self.at("end")
        for m in self.members:
            while m.steps:
                m.step()
            m.finish()


PLAN = dict(
    waiting=(),
    shared=(0, 1),
    arriving=(),
    h0p0=(2, 0),
    h0p2=(2, 3, 0, 1),
    h0=(),
    h1p0=(3, 0),
    h1p2=(1,),
    h1=(3,),
    h2p0=(2, 0, 4),
    h2p2=(3, 1, 5, 6, 2),
    h2=(3, 4),
    led=(2, 5),
    crossing=(7, 3, 4, 6),
    told=(5, 7, 0),
    end=(2, 1, 6, 4, 5, 7, 6, 7, 1),
)


class Everyone:
    def __init__(self, links, buf, me, count, device):
        self.links, self.buf, self.me, self.count, self.device = links, buf, me, count, device
        self.base = links.take(count)

    def _copy(self, j):
        slot = self.buf.at[self.me]
        peer = self.me + j
        peer = self.device(jnp.where(peer >= self.count, peer - self.count, peer))
        return self.links.copy(slot, slot, self.base + j, dp=peer)

    def _loop(self, act):
        def one(j, carry):
            act(j)
            return carry

        lax.fori_loop(1, self.count, one, 0)

    def start(self, values):
        self.buf[self.me] = values
        self._loop(lambda j: self._copy(j).start())

    def _hear(self, j):
        peer = self.me - j
        peer = jnp.where(peer < 0, peer + self.count, peer)
        self.links.arrived(self.buf.at[peer], self.base + j, dp=self.device(peer))

    def result(self):
        self._loop(self._hear)
        return lax.fori_loop(1, self.count, lambda j, acc: acc + self.buf[j], self.buf[0])

    def finish(self):
        self._loop(lambda j: self._copy(j).wait_send())


def greet(here):
    barrier = pltpu.get_barrier_semaphore()
    for axis, me, count in (("tensor", here.t, here.tensor), ("dp", here.d, here.dp)):

        def one(j, carry, axis=axis, me=me, count=count):
            peer = me + j
            peer = here.logical(**{axis: jnp.where(peer >= count, peer - count, peer)})
            pl.semaphore_signal(barrier, inc=1, device_id=peer, device_id_type=LOGICAL)
            return carry

        lax.fori_loop(1, count, one, 0)


def await_greetings(amount):
    pl.semaphore_wait(pltpu.get_barrier_semaphore(), amount)


def halves(rows):
    first = round_up(rows // 2, 16)
    return ((0, first), (first, rows - first))


def head_masks(shape, local_heads):
    lane = lax.broadcasted_iota(jnp.int32, shape, 1)
    return [
        jnp.where((lane >= h * HEAD_DIM) & (lane < (h + 1) * HEAD_DIM), 1.0, 0.0)
        for h in range(local_heads)
    ], lane


def kernel(n, S):
    here = Here(n.dp, 4)
    t, d = here.t, here.d
    here.peers = peers = [flipped(here, 1, 0), flipped(here, 1, 1), flipped(here, 0, 1)]
    links = Links(here, S.send, S.recv)
    greet(here)
    R, own, W, H, D, K = n.R, n.own, n.W, n.H, n.D, n.K
    split = halves(R)
    vector = lambda ref: ref[...].reshape(1, D)

    fetch = pltpu.make_async_copy(S.cot, S.gt, S.local.at[0])
    load = [
        pltpu.make_async_copy(getattr(S, name + "_far"), getattr(S, name), S.local.at[1 + j])
        for j, name in enumerate(LOADED)
    ]
    fetch.start()
    for copy in load:
        copy.start()
    S.a1[t] = jnp.zeros((R, D), low)
    S.cot4[t] = jnp.zeros((R, D), low)
    S.a24[t] = jnp.zeros((R, D), low)
    S.hl4[t] = jnp.zeros((R, D), low)
    rows_in = Gather(links, S.a1, here, split)
    cot_in = Gather(links, S.cot4, here, split)
    ow_in = Gather(links, S.ow4, here, ((0, W),))
    for p, (start, size) in enumerate(split):
        rows = pl.ds(start, min(size, own - start))
        unit, _ = standardize(S.x[rows, :].astype(wide))
        S.a1[t, rows, :] = (unit * vector(S.g1) + vector(S.b1)).astype(low)
        if p == 0:
            await_greetings(3 + n.dp - 1)
        rows_in.start([p])
    load[0].wait()
    S.ow4[t] = S.ow[...]
    ow_in.start()
    fetch.wait()
    S.cot4[t, 0:own, :] = S.gt[...].astype(low)
    cot_in.start([0])
    load[2].wait()
    load[3].wait()
    S.gw[0:D, :] = jnp.transpose(S.wup[...])
    S.gw[D:, :] = jnp.transpose(S.wdn[...])
    load[1].wait()
    S.v[4 * R :, :] = jnp.zeros((K - 4 * R, H), low)
    length = S.lengths[0]

    chip = here.chip

    def project(i, carry):
        s = flipped(here, *two_bits(i))

        @pl.when(i == 1)
        def _():
            rows_in.wait_sib()

        @pl.when(i == 2)
        def _():
            rows_in.forward()

        @pl.when(i == 3)
        def _():
            rows_in.wait_diag()

        slab = S.a1[s]
        lane = lax.broadcasted_iota(jnp.int32, (R, H - W), 1)
        row = lax.broadcasted_iota(jnp.int32, (R, H - W), 0)
        absent = (row >= own) | (row + s * own >= length)
        at = pl.ds(pl.multiple_of(s * R, 16), R)
        out = dot_rows(slab, S.wqkv[0]) + S.bq[0:1, :]
        S.q[s, :, :W] = (out.astype(low).astype(wide) * HEAD_DIM**-0.5).astype(low)
        S.q[s, :, W:] = jnp.where(lane == 0, HEAD_DIM**-0.5, 0.0).astype(low)
        S.k[at, :W] = dot_rows(slab, S.wqkv[1]).astype(low)
        S.k[at, W:] = jnp.where((lane == 0) & absent, -8e30, 0.0).astype(low)
        S.v[at, :W] = (dot_rows(slab, S.wqkv[2]) + S.bq[1:2, :]).astype(low)
        S.v[at, W:] = jnp.where(lane < 2, 1.0, 0.0).astype(low)
        return carry

    lax.fori_loop(0, 4, project, 0)
    if K > 4 * R:
        lane = lax.broadcasted_iota(jnp.int32, (K - 4 * R, H), 1)
        S.k[4 * R :, :] = jnp.where(lane == W, -8e30, 0.0).astype(low)
    S.kt[...] = jnp.transpose(S.k[...])
    S.vt[...] = jnp.transpose(S.v[...])

    masks, lane = head_masks((1, H), n.heads)
    mix_base = links.take(3)


    def attend(i, carry):
        high, low_bit = two_bits(i)
        s = flipped(here, 1 - high, low_bit + high - 2 * low_bit * high)
        query = S.q[s]
        mixed = jnp.zeros((R, H), wide)
        inverse = jnp.zeros((R, 128), wide)
        first = lax.broadcasted_iota(jnp.int32, (1, 128), 1)

        def score(h):
            here = jnp.where(lane == W, 1.0, masks[h]).astype(low)
            return dot(query * here, S.kt[...])

        ready = score(0)
        for h in range(n.heads):
            scores = ready
            if h + 1 < n.heads:
                ready = score(h + 1)
            terms = jnp.exp(scores - jnp.max(scores, -1, keepdims=True)).astype(low)
            S.e[h, s] = terms
            part = dot(terms, S.v[...])
            scale = 1.0 / part[:, W : W + 1]
            mixed += part * (scale * masks[h])
            inverse = jnp.where(first == h, scale, inverse)
        S.o[s] = mixed
        S.inv[s] = inverse
        S.mix[s] = mixed[:, :W].astype(low)

        @pl.when(i < 3)
        def _():
            links.copy(S.mix.at[s], S.mix4.at[t], mix_base + i, tensor=s).start()

        @pl.when(i == 1)
        def _():
            cot_in.start([1])

        @pl.when(i == 2)
        def _():
            ow_in.wait_sib()
            ow_in.forward()

        return carry

    lax.fori_loop(0, 4, attend, 0)
    ow_in.wait_diag()
    S.mix4[t] = S.mix[t]
    for j, s in enumerate(peers):
        links.arrived(S.mix4.at[s], mix_base + j, tensor=s)

    total = dot(S.mix4[0], S.ow4[0])
    for j in range(1, 4):
        total += dot(S.mix4[j], S.ow4[j])
    total = S.x[...].astype(wide) + (total[:own] + vector(S.ob))
    S.hid[...] = total
    unit, _ = standardize(total)
    S.a24[t, 0:own, :] = (unit * vector(S.g2) + vector(S.b2)).astype(low)
    next_in = Gather(links, S.a24, here, halves(R))
    next_in.start()
    back = Reduce(links, S.part, S.pre1, S.near1, S.far1, here, split)
    ahead = Reduce(links, S.fop, S.pre2, S.near2, S.far2, here, split)
    S.gub[...] = jnp.zeros_like(S.gub)

    def feed(s, start, size):
        rows = pl.ds(start, size)
        up = dot(S.a24[s, rows], S.wup[...]) + vector(S.bup)
        square = up * up
        c = 0.7978845608028654
        bend = jnp.tanh(c * up * (1.0 + 0.044715 * square))
        half = 0.5 * (1.0 + bend)
        slope = half + 0.5 * up * (1.0 - bend * bend) * (c + (3 * 0.044715 * c) * square)
        active = (up * half).astype(low)
        S.pool[s, rows, 0:D] = active
        grad = (dot(S.cot4[s, rows], S.gw[D:, :]) * slope).astype(low)
        S.gup[s, rows] = grad
        S.part[s, rows] = dot(grad, S.gw[0:D, :]).astype(low)
        S.gub[...] += jnp.sum(grad.astype(wide), 0, keepdims=True)

    def lead_out(s, start, size):
        rows = pl.ds(start, size)
        S.fop[s, rows] = dot(S.pool[s, rows, 0:D], S.wdn[...]).astype(low)

    def feed_here(i, carry):
        s = flipped(here, 0, i)

        @pl.when(i == 1)
        def _():
            next_in.wait_sib()
            cot_in.wait_sib()

        feed(s, 0, R)

        @pl.when(i == 1)
        def _():
            back.send_sib()

        lead_out(s, 0, R)
        return carry

    lax.fori_loop(0, 2, feed_here, 0)
    ahead.send_sib()
    for p in (0, 1):

        def feed_there(i, carry, p=p):
            @pl.when(i == 0)
            def _():
                cot_in.forward([p])
                next_in.forward([p])

            @pl.when(i == 1)
            def _():
                cot_in.wait_diag([p])
                next_in.wait_diag([p])

            feed(flipped(here, 1, i), *split[p])
            if p == 1:

                @pl.when(i == 0)
                def _():
                    back.send_cross([0])

            return carry

        lax.fori_loop(0, 2, feed_there, 0)
        back.send_diag([p])
    for i in (0, 1):
        lead_out(flipped(here, 1, i), 0, R)
    back.send_cross([1])
    ahead.send_diag()

    sums = Pipeline(PLAN)
    tile = D // 2
    box_at = 0

    def sum_over_dp(kind, held, whole, out, first, rows):
        nonlocal box_at
        sums.add(kind(links, held, whole, out, S.box, box_at, first, rows))
        box_at += kind.sizes(rows, D, n.dp)[1]

    for left, right, first in ((S.a24, S.gup, 0), (S.pool, S.cot4, D)):
        rows = left[:, :, 0:D].reshape(4 * R, D)
        S.gw[first : first + D, :] = dot_columns(rows, flat(right)).astype(low)
        for at in (first, first + tile):
            kind = Halves if at == tile else HalvesFromX
            sum_over_dp(kind, S.gw, S.sum1, S.whole1, at, tile)

    sums.at("waiting")
    S.small[...] = jnp.zeros_like(S.small)
    gm_base = links.take(6)
    shared = lambda s, p, j: links.copy(
        S.mix4.at[s, pl.ds(*split[p])], S.gm4.at[t, pl.ds(*split[p])], gm_base + 3 * p + j, tensor=peers[j]
    )
    for p, (start, size) in enumerate(split):
        real = min(size, own - start)
        rows = pl.ds(start, real)
        grad = back.result(p)[:real]
        unit, inverse = standardize(S.hid[rows])
        S.small[2:3, :] += jnp.sum(grad * unit, 0, keepdims=True)
        S.small[3:4, :] += jnp.sum(grad, 0, keepdims=True)
        S.gt[rows] += norm_back(grad, unit, inverse, vector(S.g2))
        S.hl4[t, rows] = S.gt[rows].astype(low)
        rows = pl.ds(start, size)
        for j, s in enumerate(peers + [t]):
            product = dot_rows(S.hl4[t, rows], S.ow4[s]).astype(low)
            if j < 3:
                S.mix4[s, rows] = product
                shared(s, p, j).start()
            else:
                S.gm4[t, rows] = product
    S.small[4:5, :] = jnp.sum(S.hl4[t].astype(wide), 0, keepdims=True)
    S.small[5:6, :] = jnp.sum(S.cot4[t].astype(wide), 0, keepdims=True)
    S.small[6:7, :] = S.gub[...]
    hl_in = Gather(links, S.hl4, here, halves(R))

    next_in.finish()
    S.do[...] = jnp.zeros_like(S.do)
    S.qt[...] = jnp.transpose(flat(S.q))
    sums.at("shared")

    def prepare(i, s):
        if i > 0:
            j = (None, 2, 0, 1)[i]
            for p in (0, 1):
                rows = pl.ds(*split[p])
                links.arrived(S.gm4.at[s, rows], gm_base + 3 * p + j, tensor=peers[j])
        S.do[:, :W] = S.gm4[s].astype(wide)
        inverse = sum(S.inv[s, :, h : h + 1] * masks[h] for h in range(n.heads))
        scaled = (S.do[...] * inverse).astype(low)
        S.v[pl.ds(pl.multiple_of(s * R, 16), R), :] = scaled
        scaled = scaled.astype(wide)
        product = scaled * S.o[s]
        for h in range(n.heads):
            inner = -jnp.sum(product * masks[h], -1, keepdims=True)
            upper = inner.astype(low).astype(wide)
            S.a24[s, :, h * H : (h + 1) * H] = (
                scaled * masks[h]
                + jnp.where(lane == W, upper, 0.0)
                + jnp.where(lane == W + 1, inner - upper, 0.0)
            ).astype(low)

    def pull(h, p):
        grad_p = dot(pair(S.a24.at[:, :, h * H : (h + 1) * H], p), S.vt[...])
        grad_s = (pair(S.e.at[h], p).astype(wide) * grad_p).astype(low)
        set_pair(S.pool, p, grad_s)
        dq = dot(grad_s, S.k[...]) * (masks[h] * HEAD_DIM**-0.5)
        if h > 0:
            dq += pair(S.gup.at[:, :, 0:H], p).astype(wide)
        S.gup[pl.ds(2 * p, 2), :, 0:H] = dq.astype(low).reshape(2, R, H)

    def weights(h):
        at = slice(h * HEAD_DIM, (h + 1) * HEAD_DIM)
        tile = h * HEAD_DIM // 128 * 128
        dqt = jnp.transpose(flat(S.gup.at[:, :, tile : tile + 128]))
        left = jnp.concatenate(
            [dqt[h * HEAD_DIM - tile : (h + 1) * HEAD_DIM - tile], S.qt[at, :], S.kt[at, : 4 * R]], 0
        )
        out = dot(left, flat(S.a1))
        S.gw2[h * W : (h + 1) * W, :] = out.astype(low)
        for c in range(3):
            product = out[c * HEAD_DIM : (c + 1) * HEAD_DIM] * S.wqkv[c, at, :].astype(wide)
            S.small[0:1, :] += jnp.sum(product, 0, keepdims=True)
        sum_over_dp(Quarters, S.gw2, S.sum2, S.whole2, h * W, W)

    for h in range(n.heads):
        for i in (0, 2):
            if (h, i) == (0, 2):
                sums.at("arriving")
            if h == 0:
                prepare(i, flipped(here, i // 2, 0))
                prepare(i + 1, flipped(here, i // 2, 1))
            if (h, i) == (0, 2):
                hl_in.start()
            pull(h, chip if i == 0 else 1 - chip)
            sums.at(f"h{h}p{i}")
            if (h, i) == (1, 0):
                hl_in.wait_sib()
                hl_in.forward()
                ahead.send_cross()
            elif (h, i) == (1, 2):
                hl_in.wait_diag()
                S.gw2[3 * W :, :] = dot_columns(flat(S.mix), flat(S.hl4)).astype(low)
                sum_over_dp(Quarters, S.gw2, S.sum2, S.whole2, 3 * W, W)
        if h == 0:
            S.v[4 * R :, :] = jnp.zeros((K - 4 * R, H), low)
            S.kt[...] = jnp.transpose(S.v[...])
        at = slice(h * HEAD_DIM, (h + 1) * HEAD_DIM)
        S.qt[at, :] = dot(S.qt[at, :], flat(S.pool))[:, : 4 * R].astype(low)
        S.kt[at, : 4 * R] = dot(S.kt[at, : 4 * R], flat(S.e.at[h]))[:, : 4 * R].astype(low)
        if h + 1 < n.heads:
            weights(h)
        sums.at(f"h{h}")

    pad = jnp.zeros((R, H - W), low)
    for part, grad_t in ((1, S.qt), (2, S.kt)):
        rows = jnp.transpose(grad_t[:W, : 4 * R])
        for s in range(4):
            S.gup[s, :, part * H : part * H + W] = rows[s * R : (s + 1) * R]
            S.gup[s, :, part * H + W : (part + 1) * H] = pad

    back.finish()
    down = Reduce(links, S.part, S.pre1, S.near1, S.far1, here, split)

    def lead(s, start, size):
        rows = pl.ds(start, size)
        out = dot(S.gup[s, rows, 0:W], S.wqkv[0])
        out += dot(S.gup[s, rows, H : H + W], S.wqkv[1])
        out += dot(S.gup[s, rows, 2 * H : 2 * H + W], S.wqkv[2])
        S.part[s, rows] = out.astype(low)

    cross, diag, sib = peers
    lead(diag, *split[0])
    down.send_diag([0])
    lead(cross, *split[0])
    weights(n.heads - 1)
    down.send_cross([0])
    lead(diag, *split[1])
    down.send_diag([1])
    lead(cross, *split[1])
    down.send_cross([1])
    lead(sib, 0, R)
    down.send_sib()
    lead(t, 0, R)
    columns = jnp.sum(flat(S.gup).astype(wide), 0, keepdims=True)
    S.small[7:8, 0:H] = columns[:, 0:H]
    S.small[7:8, H : 2 * H] = columns[:, 2 * H :]
    upper = columns.astype(low)
    both = jnp.concatenate([upper.astype(wide), columns - upper.astype(wide)], 0).astype(low)
    for c in range(3):
        product = dot(both[:, c * H : c * H + W], S.wqkv[c])
        S.small[1:2, :] += jnp.sum(product, 0, keepdims=True)

    S.small4[t] = S.small[...]
    base3 = links.take(3)
    for j in range(3):
        links.start(S.small4.at[t], S.small4.at[t], base3 + j, tensor=peers[j])
    sums.at("led")
    result = jnp.concatenate([ahead.result(0), ahead.result(1)], 0)
    S.output[...] = (S.hid[...] + (result[:own] + vector(S.db))).astype(low)
    sums.at("crossing")

    unit, inverse = standardize(S.x[...].astype(wide))
    grad = jnp.concatenate([down.result(0), down.result(1)], 0)[:own]
    for j in range(3):
        links.arrived(S.small4.at[peers[j]], base3 + j, tensor=peers[j])
    over = S.small4[0] + S.small4[1] + S.small4[2] + S.small4[3]
    row = lax.broadcasted_iota(jnp.int32, over.shape, 0)
    near = min(8, n.dp)
    inner = Everyone(links, S.smalls, here.near, near, lambda j: here.group + j)
    inner.start(jnp.where(row < 6, over, S.small[...]))
    S.gt[...] += norm_back(grad, unit, inverse, vector(S.g1))
    sums.at("told")
    sums.finish()
    total = inner.result()
    inner.finish()
    if n.dp > near:
        outer = Everyone(links, S.smalls2, lax.div(here.group, near), n.dp // near, lambda j: j * near + here.near)
        outer.start(total)
        total = outer.result()
        outer.finish()
    S.small_sum[...] = total
    S.small_sum[0:1, :] = (total[0:1, :] - vector(S.b1) * total[1:2, :]) / vector(S.g1)
    for j, s in enumerate(peers):
        links.copy(S.mix.at[s], S.mix4.at[t], mix_base + j, tensor=s).wait_send()
        for p in (0, 1):
            shared(s, p, j).wait_send()
    for transfer in (rows_in, cot_in, ow_in, hl_in, ahead, down):
        transfer.finish()
    links.finish()


LOADED = ("ow", "wqkv", "wup", "wdn")
SMALL = ("gain1", "shift1", "gain2", "shift2", "bias_out", "bias_down", "bias_up", "bias_qv")


def finish(n, output, gt, small, whole1, whole2):
    D, W, H = n.D, n.W, n.H
    steps = n.heads
    rows1 = D // steps

    def spread(output, gt, small, up, down, head, out, *refs):
        to_output, to_gt, to_up, to_down, to_qkv, to_out = refs[:6]
        vectors, sems = refs[6:14], refs[14]
        i = pl.program_id(0)
        held = refs[15:]
        come = [pltpu.make_async_copy(a, b, sems.at[j]) for j, (a, b) in enumerate(zip((output, gt), held))]
        go = [
            pltpu.make_async_copy(a, b, sems.at[2 + j])
            for j, (a, b) in enumerate(zip(held, (to_output, to_gt)))
        ]

        @pl.when(i == 0)
        def _():
            for copy in come:
                copy.start()
            for j in range(7):
                vectors[j][...] = small[j : j + 1, :].reshape(D)
            vectors[7][0:1, :] = small[7:8, :W]
            vectors[7][1:2, :] = small[7:8, H : H + W]

        to_up[...] = up[...].astype(wide)
        to_down[...] = down[...].astype(wide)
        for j in range(3):
            to_qkv[j] = head[j * HEAD_DIM : (j + 1) * HEAD_DIM, :].astype(wide)
        to_out[...] = out[...].astype(wide)

        @pl.when(i == 1)
        def _():
            for first, second in zip(come, go):
                first.wait()
                second.start()

        @pl.when(i == steps - 1)
        def _():
            for copy in go:
                copy.wait()

    hbm = pl.BlockSpec(memory_space=pl.ANY)
    whole = pl.BlockSpec(memory_space=pltpu.VMEM)
    at_row = lambda rows, index: pl.BlockSpec((rows, D), lambda i: (index(i), 0))
    shape = jax.ShapeDtypeStruct
    return pl.pallas_call(
        spread,
        grid=(steps,),
        out_shape=[shape(output.shape, low), shape(gt.shape, wide)]
        + [shape((D, D), wide)] * 2
        + [shape((3, W, D), wide), shape((W, D), wide)]
        + [shape((D,), wide)] * 7
        + [shape((2, W), wide)],
        in_specs=[hbm, hbm, whole, at_row(rows1, lambda i: i), at_row(rows1, lambda i: i + steps)]
        + [at_row(W, lambda i: i), at_row(HEAD_DIM, lambda i: 3 * steps + i)],
        out_specs=[hbm, hbm]
        + [at_row(rows1, lambda i: i)] * 2
        + [pl.BlockSpec((3, HEAD_DIM, D), lambda i: (0, i, 0)), at_row(HEAD_DIM, lambda i: i)]
        + [whole] * 8,
        scratch_shapes=[
            pltpu.SemaphoreType.DMA((4,)),
            pltpu.VMEM(output.shape, low),
            pltpu.VMEM(gt.shape, wide),
        ],
    )(output, gt, small, whole1, whole1, whole2, whole2)


def body(
    tokens,
    lengths,
    ln1_gain,
    ln1_shift,
    qkv_weight,
    qv_bias,
    out_weight,
    out_bias,
    ln2_gain,
    ln2_shift,
    up_weight,
    up_bias,
    down_weight,
    down_bias,
    cotangent,
):
    own, D = tokens.shape
    W = qkv_weight.shape[2]
    F = up_weight.shape[1]
    dp = lax.axis_size("dp")
    assert lax.axis_size("tensor") == 4 and lengths.shape[0] == 1 and F == D and 4 * W == D and 3 * round_up(W + 2, 128) == D
    R = round_up(own, 16)
    H = round_up(W + 2, 128)
    K = round_up(4 * R, 256)
    heads = W // HEAD_DIM
    extra = dp.bit_length() - 1 - 3
    n = types.SimpleNamespace(
        own=own, D=D, W=W, R=R, H=H, K=K, dp=dp, heads=heads, extra=extra
    )
    weights = dict(ow=out_weight, wqkv=jnp.transpose(qkv_weight, (1, 2, 0)), wup=up_weight, wdn=down_weight)
    given = dict(
        x=tokens, lengths=lengths, g1=ln1_gain, b1=ln1_shift,
        bq=qv_bias, ob=out_bias, g2=ln2_gain, b2=ln2_shift, bup=up_bias, db=down_bias,
        cot=cotangent,
    )
    given.update({name + "_far": weights[name] for name in LOADED})
    outs = dict(
        output=((own, D), low), gt=((own, D), wide), small_sum=((8, D), wide),
        whole1=((2 * D, D), low), whole2=((D, D), low),
    )
    rows4 = ((4, R, D), low)
    slab = ((R, D), low)
    chunks = [(Halves, D // 2)] * 4 + [(Quarters, W)] * 4
    scratch = dict(
        a1=rows4, cot4=rows4, ow4=((4, W, D), low), q=((4, R, H), low), k=((K, H), low),
        v=((K, H), low), kt=((H, K), low), vt=((H, K), low), e=((heads, 4, R, K), low),
        o=((4, R, H), wide), inv=((4, R, 128), wide), mix=((4, R, W), low), mix4=((4, R, W), low),
        hid=((own, D), wide),
        a24=rows4, pool=((4, R, K), low), gup=rows4, part=rows4,
        fop=rows4, pre1=slab, near1=slab, far1=slab, pre2=slab, near2=slab, far2=slab,
        gw=((2 * D, D), low), gub=((1, D), wide),
        small=((8, D), wide), hl4=rows4,
        gm4=((4, R, W), low), qt=((H, 4 * R), low), do=((R, H), wide),
        gw2=((D, D), low),
        small4=((4, 8, D), wide), smalls=((min(8, dp), 8, D), wide),
        box=((sum(kind.sizes(r, D, dp)[1] for kind, r in chunks), D), low),
        sum1=((2 * D, D), low), sum2=((D, D), low),
    )
    scratch.update({name: (weights[name].shape, low) for name in LOADED})
    if dp > 8:
        scratch["smalls2"] = ((dp // 8, 8, D), wide)
    sems = 170 + dp + 8 * extra
    names = list(given) + list(outs) + list(scratch) + ["local", "send", "recv"]
    vmem = pl.BlockSpec(memory_space=pltpu.VMEM)
    smem = pl.BlockSpec(memory_space=pltpu.SMEM)
    hbm = pl.BlockSpec(memory_space=pl.ANY)
    output, gt, small, whole1, whole2 = pl.pallas_call(
        lambda *refs: kernel(n, types.SimpleNamespace(**dict(zip(names, refs)))),
        out_shape=tuple(jax.ShapeDtypeStruct(*spec) for spec in outs.values()),
        in_specs=[
            hbm if name.endswith("_far") else dict(lengths=smem, cot=hbm).get(name, vmem) for name in given
        ],
        out_specs=tuple(hbm if name in ("whole1", "whole2") else vmem for name in outs),
        scratch_shapes=[pltpu.VMEM(*spec) for spec in scratch.values()]
        + [pltpu.SemaphoreType.DMA((5,))] + [pltpu.SemaphoreType.DMA((sems,))] * 2,
        compiler_params=pltpu.CompilerParams(
            collective_id=0, has_side_effects=True, vmem_limit_bytes=VMEM_BYTES
        ),
    )(*given.values())
    finished = finish(n, output, gt, small, whole1, whole2)
    small_rows = dict(zip(SMALL, finished[6:]))
    return (
        finished[0],
        finished[1],
        small_rows["gain1"],
        small_rows["shift1"],
        jnp.transpose(finished[4], (2, 0, 1)),
        small_rows["bias_qv"],
        finished[5],
        small_rows["bias_out"],
        small_rows["gain2"],
        small_rows["shift2"],
        finished[2],
        small_rows["bias_up"],
        finished[3],
        small_rows["bias_down"],
    )


def solution(mesh):
    placed = (
        P(("dp", "tensor"), None),
        P("dp"),
        P(),
        P(),
        P(None, None, "tensor"),
        P(None, "tensor"),
        P("tensor", None),
        P(),
        P(),
        P(),
        P(None, "tensor"),
        P("tensor"),
        P("tensor", None),
        P(),
        P(("dp", "tensor"), None),
    )
    return jax.shard_map(
        body,
        mesh=mesh,
        in_specs=placed,
        out_specs=(
            P(("dp", "tensor"), None),
            P(("dp", "tensor"), None),
            P(),
            P(),
            P(None, None, "tensor"),
            P(None, "tensor"),
            P("tensor", None),
            P(),
            P(),
            P(),
            P(None, "tensor"),
            P("tensor"),
            P("tensor", None),
            P(),
        ),
        check_vma=False,
    )
```

profile of v0, /device:TPU:0, one launch (start us, length us, event | category | flops | bytes accessed | tf_op | source)
XLA Modules:
  0.0 150.1 jit_solution(12158539448021814103)
XLA Ops:
  1.3 142.8 %shard_map.254 = (bf16[298,768]{1,0:T(8,128)(2,1)}, f32[298,768]{1,0:T(8,128)}, f32[8,768]{1,0:T(8,128)}, bf16[1536,768]{1,0:T(8,128)(2,1)}, bf16[768,768]{1,0:T(8,128)(2,1)}) custom-call(bf16[298,768]{1,0:T(8,128)(2,1)} %refs_0_.1, s32[1]{0:T(128)S(6)} %copy.29.refs_1_, f32[768]{0:T(1024)} %refs_2_.1, f32[768]{0:T(1024)} %refs_3_.1, f32[2,192]{1,0:T(2,128)} %refs_4_.1, ...), custom_call_target="tpu_custom_call" | custom-call | tf_op jit(solution)/shard_map/pallas_call | solution.py:1078
  144.1 5.8 %shard_map.255 = (bf16[298,768]{1,0:T(8,128)(2,1)}, f32[298,768]{1,0:T(8,128)}, f32[768,768]{1,0:T(8,128)}, f32[768,768]{1,0:T(8,128)}, f32[3,192,768]{2,1,0:T(8...) custom-call(bf16[298,768]{1,0:T(8,128)(2,1)} %get-tuple-element.33.o, ...), custom_call_target="tpu_custom_call" | custom-call | tf_op jit(solution)/shard_map/pallas_call | solution.py:989
where the time goes:
time: 150 us
  Pallas kernels  149 us (99%)
    pallas_call x1, Pallas kernels, body(): pl.pallas_call(lambda *refs: kernel(n, types.SimpleNamespace(**dict(zip(n...  143 us
    pallas_call x1, Pallas kernels, finish(): pl.pallas_call(spread, grid=(steps,), out_shape=[shape(output.shape, low)...  5.82 us

commit v1 on v0

--- a/solution.py
+++ b/solution.py
@@ -437,21 +437,21 @@
 
 PLAN = dict(
     waiting=(),
-    shared=(0, 1),
+    shared=(1, 0),
     arriving=(),
-    h0p0=(2, 0),
-    h0p2=(2, 3, 0, 1),
-    h0=(),
-    h1p0=(3, 0),
-    h1p2=(1,),
-    h1=(3,),
-    h2p0=(2, 0, 4),
-    h2p2=(3, 1, 5, 6, 2),
-    h2=(3, 4),
-    led=(2, 5),
-    crossing=(7, 3, 4, 6),
-    told=(5, 7, 0),
-    end=(2, 1, 6, 4, 5, 7, 6, 7, 1),
+    h0p0=(2, 1),
+    h0p2=(2, 3),
+    h0=(1,),
+    h1p0=(2, 4),
+    h1p2=(3,),
+    h1=(4, 2, 6, 3, 0),
+    h2p0=(2, 4, 1),
+    h2p2=(6, 5),
+    h2=(),
+    led=(3, 2, 1, 4, 0, 6, 7, 5),
+    crossing=(3, 1, 4, 0, 6),
+    told=(3, 7, 4, 5),
+    end=(0, 6, 7, 5, 6, 7, 0),
 )
 
 
@@ -749,7 +749,7 @@
         rows = left[:, :, 0:D].reshape(4 * R, D)
         S.gw[first : first + D, :] = dot_columns(rows, flat(right)).astype(low)
         for at in (first, first + tile):
-            kind = Halves if at == tile else HalvesFromX
+            kind = Halves if at == 0 else HalvesFromX
             sum_over_dp(kind, S.gw, S.sum1, S.whole1, at, tile)
 
     sums.at("waiting")
@@ -827,7 +827,8 @@
         for c in range(3):
             product = out[c * HEAD_DIM : (c + 1) * HEAD_DIM] * S.wqkv[c, at, :].astype(wide)
             S.small[0:1, :] += jnp.sum(product, 0, keepdims=True)
-        sum_over_dp(Quarters, S.gw2, S.sum2, S.whole2, h * W, W)
+        kind = HalvesFromX if h + 1 < n.heads else Quarters
+        sum_over_dp(kind, S.gw2, S.sum2, S.whole2, h * W, W)
 
     for h in range(n.heads):
         for i in (0, 2):
@@ -1051,7 +1052,7 @@
     )
     rows4 = ((4, R, D), low)
     slab = ((R, D), low)
-    chunks = [(Halves, D // 2)] * 4 + [(Quarters, W)] * 4
+    chunks = [(Halves, D // 2)] * 4 + [(Halves, W)] * 2 + [(Quarters, W)] * 2
     scratch = dict(
         a1=rows4, cot4=rows4, ow4=((4, W, D), low), q=((4, R, H), low), k=((K, H), low),
         v=((K, H), low), kt=((H, K), low), vt=((H, K), low), e=((heads, 4, R, K), low),
@@ -1070,7 +1071,7 @@
     scratch.update({name: (weights[name].shape, low) for name in LOADED})
     if dp > 8:
         scratch["smalls2"] = ((dp // 8, 8, D), wide)
-    sems = 170 + dp + 8 * extra
+    sems = 180 + dp + 8 * extra
     names = list(given) + list(outs) + list(scratch) + ["local", "send", "recv"]
     vmem = pl.BlockSpec(memory_space=pltpu.VMEM)
     smem = pl.BlockSpec(memory_space=pltpu.SMEM)

time: 150 us -> 156 us (1.040)
  Pallas kernels: 149 us -> 154 us
    pallas_call x1, Pallas kernels: 143 us -> 148 us  [body(): pl.pallas_call(lambda *refs: kernel(n, types.SimpleNamespace(**dict(zip(n...]
where the time goes in v1:
time: 156 us
  Pallas kernels  154 us (99%)
    pallas_call x1, Pallas kernels, body(): pl.pallas_call(lambda *refs: kernel(n, types.SimpleNamespace(**dict(zip(n...  148 us
    pallas_call x1, Pallas kernels, finish(): pl.pallas_call(spread, grid=(steps,), out_shape=[shape(output.shape, low)...  5.82 us

profile of v1, /device:TPU:0, one launch (start us, length us, event | category | flops | bytes accessed | tf_op | source)
XLA Modules:
  0.0 155.7 jit_solution(3308960056820055507)
XLA Ops:
  1.3 148.4 %shard_map.254 = (bf16[298,768]{1,0:T(8,128)(2,1)}, f32[298,768]{1,0:T(8,128)}, f32[8,768]{1,0:T(8,128)}, bf16[1536,768]{1,0:T(8,128)(2,1)}, bf16[768,768]{1,0:T(8,128)(2,1)}) custom-call(bf16[298,768]{1,0:T(8,128)(2,1)} %refs_0_.1, s32[1]{0:T(128)S(6)} %copy.29.refs_1_, f32[768]{0:T(1024)} %refs_2_.1, f32[768]{0:T(1024)} %refs_3_.1, f32[2,192]{1,0:T(2,128)} %refs_4_.1, ...), custom_call_target="tpu_custom_call" | custom-call | tf_op jit(solution)/shard_map/pallas_call | solution.py:1079
  149.7 5.8 %shard_map.255 = (bf16[298,768]{1,0:T(8,128)(2,1)}, f32[298,768]{1,0:T(8,128)}, f32[768,768]{1,0:T(8,128)}, f32[768,768]{1,0:T(8,128)}, f32[3,192,768]{2,1,0:T(8...) custom-call(bf16[298,768]{1,0:T(8,128)(2,1)} %get-tuple-element.33.o, ...), custom_call_target="tpu_custom_call" | custom-call | tf_op jit(solution)/shard_map/pallas_call | solution.py:990

commit v2 on v0

--- a/solution.py
+++ b/solution.py
@@ -437,21 +437,21 @@
 
 PLAN = dict(
     waiting=(),
-    shared=(0, 1),
-    arriving=(),
-    h0p0=(2, 0),
-    h0p2=(2, 3, 0, 1),
-    h0=(),
-    h1p0=(3, 0),
+    shared=(0,),
+    arriving=(2, 0),
+    h0p0=(),
+    h0p2=(2, 1, 3, 0),
+    h0=(1, 3, 2),
+    h1p0=(0,),
     h1p2=(1,),
-    h1=(3,),
-    h2p0=(2, 0, 4),
-    h2p2=(3, 1, 5, 6, 2),
-    h2=(3, 4),
-    led=(2, 5),
-    crossing=(7, 3, 4, 6),
-    told=(5, 7, 0),
-    end=(2, 1, 6, 4, 5, 7, 6, 7, 1),
+    h1=(3, 4, 0, 2, 6, 5),
+    h2p0=(1,),
+    h2p2=(3, 7, 2, 0, 6, 4, 5),
+    h2=(3,),
+    led=(6, 2, 8, 7, 5, 4),
+    crossing=(6, 3, 8),
+    told=(1,),
+    end=(4, 6, 5, 7, 8, 6, 7, 1, 8),
 )
 
 
@@ -815,19 +815,20 @@
             dq += pair(S.gup.at[:, :, 0:H], p).astype(wide)
         S.gup[pl.ds(2 * p, 2), :, 0:H] = dq.astype(low).reshape(2, R, H)
 
+    def keep(out, row, parts):
+        S.gw2[row : row + out.shape[0], :] = out.astype(low)
+        for j, (c, h) in enumerate(parts):
+            product = out[j * HEAD_DIM : (j + 1) * HEAD_DIM]
+            product *= S.wqkv[c, h * HEAD_DIM : (h + 1) * HEAD_DIM, :].astype(wide)
+            S.small[0:1, :] += jnp.sum(product, 0, keepdims=True)
+        sum_over_dp(Quarters, S.gw2, S.sum2, S.whole2, row, out.shape[0])
+
     def weights(h):
         at = slice(h * HEAD_DIM, (h + 1) * HEAD_DIM)
         tile = h * HEAD_DIM // 128 * 128
         dqt = jnp.transpose(flat(S.gup.at[:, :, tile : tile + 128]))
-        left = jnp.concatenate(
-            [dqt[h * HEAD_DIM - tile : (h + 1) * HEAD_DIM - tile], S.qt[at, :], S.kt[at, : 4 * R]], 0
-        )
-        out = dot(left, flat(S.a1))
-        S.gw2[h * W : (h + 1) * W, :] = out.astype(low)
-        for c in range(3):
-            product = out[c * HEAD_DIM : (c + 1) * HEAD_DIM] * S.wqkv[c, at, :].astype(wide)
-            S.small[0:1, :] += jnp.sum(product, 0, keepdims=True)
-        sum_over_dp(Quarters, S.gw2, S.sum2, S.whole2, h * W, W)
+        left = jnp.concatenate([dqt[h * HEAD_DIM - tile : (h + 1) * HEAD_DIM - tile], S.qt[at, :]], 0)
+        keep(dot(left, flat(S.a1)), 2 * h * HEAD_DIM, [(0, h), (1, h)])
 
     for h in range(n.heads):
         for i in (0, 2):
@@ -847,13 +848,16 @@
             elif (h, i) == (1, 2):
                 hl_in.wait_diag()
                 S.gw2[3 * W :, :] = dot_columns(flat(S.mix), flat(S.hl4)).astype(low)
-                sum_over_dp(Quarters, S.gw2, S.sum2, S.whole2, 3 * W, W)
+                sum_over_dp(HalvesFromX, S.gw2, S.sum2, S.whole2, 3 * W, W)
+        at = slice(h * HEAD_DIM, (h + 1) * HEAD_DIM)
         if h == 0:
             S.v[4 * R :, :] = jnp.zeros((K - 4 * R, H), low)
             S.kt[...] = jnp.transpose(S.v[...])
-        at = slice(h * HEAD_DIM, (h + 1) * HEAD_DIM)
+            for g in range(n.heads):
+                rows = slice(g * HEAD_DIM, (g + 1) * HEAD_DIM)
+                S.kt[rows, : 4 * R] = dot(S.kt[rows, : 4 * R], flat(S.e.at[g]))[:, : 4 * R].astype(low)
+            keep(dot(S.kt[:W, : 4 * R], flat(S.a1)), 2 * W, [(2, g) for g in range(n.heads)])
         S.qt[at, :] = dot(S.qt[at, :], flat(S.pool))[:, : 4 * R].astype(low)
-        S.kt[at, : 4 * R] = dot(S.kt[at, : 4 * R], flat(S.e.at[h]))[:, : 4 * R].astype(low)
         if h + 1 < n.heads:
             weights(h)
         sums.at(f"h{h}")
@@ -945,7 +949,7 @@
     steps = n.heads
     rows1 = D // steps
 
-    def spread(output, gt, small, up, down, head, out, *refs):
+    def spread(output, gt, small, up, down, head, value, out, *refs):
         to_output, to_gt, to_up, to_down, to_qkv, to_out = refs[:6]
         vectors, sems = refs[6:14], refs[14]
         i = pl.program_id(0)
@@ -967,8 +971,9 @@
 
         to_up[...] = up[...].astype(wide)
         to_down[...] = down[...].astype(wide)
-        for j in range(3):
-            to_qkv[j] = head[j * HEAD_DIM : (j + 1) * HEAD_DIM, :].astype(wide)
+        to_qkv[0] = head[0:HEAD_DIM, :].astype(wide)
+        to_qkv[1] = head[HEAD_DIM:, :].astype(wide)
+        to_qkv[2] = value[...].astype(wide)
         to_out[...] = out[...].astype(wide)
 
         @pl.when(i == 1)
@@ -995,7 +1000,8 @@
         + [shape((D,), wide)] * 7
         + [shape((2, W), wide)],
         in_specs=[hbm, hbm, whole, at_row(rows1, lambda i: i), at_row(rows1, lambda i: i + steps)]
-        + [at_row(W, lambda i: i), at_row(HEAD_DIM, lambda i: 3 * steps + i)],
+        + [at_row(2 * HEAD_DIM, lambda i: i)]
+        + [at_row(HEAD_DIM, lambda i, j=j: j * steps + i) for j in (2, 3)],
         out_specs=[hbm, hbm]
         + [at_row(rows1, lambda i: i)] * 2
         + [pl.BlockSpec((3, HEAD_DIM, D), lambda i: (0, i, 0)), at_row(HEAD_DIM, lambda i: i)]
@@ -1005,7 +1011,7 @@
             pltpu.VMEM(output.shape, low),
             pltpu.VMEM(gt.shape, wide),
         ],
-    )(output, gt, small, whole1, whole1, whole2, whole2)
+    )(output, gt, small, whole1, whole1, whole2, whole2, whole2)
 
 
 def body(
@@ -1051,7 +1057,7 @@
     )
     rows4 = ((4, R, D), low)
     slab = ((R, D), low)
-    chunks = [(Halves, D // 2)] * 4 + [(Quarters, W)] * 4
+    chunks = [(Halves, D // 2)] * 4 + [(Halves, W), (Quarters, W)] + [(Quarters, 2 * HEAD_DIM)] * heads
     scratch = dict(
         a1=rows4, cot4=rows4, ow4=((4, W, D), low), q=((4, R, H), low), k=((K, H), low),
         v=((K, H), low), kt=((H, K), low), vt=((H, K), low), e=((heads, 4, R, K), low),
@@ -1070,7 +1076,7 @@
     scratch.update({name: (weights[name].shape, low) for name in LOADED})
     if dp > 8:
         scratch["smalls2"] = ((dp // 8, 8, D), wide)
-    sems = 170 + dp + 8 * extra
+    sems = 190 + dp + 9 * extra
     names = list(given) + list(outs) + list(scratch) + ["local", "send", "recv"]
     vmem = pl.BlockSpec(memory_space=pltpu.VMEM)
     smem = pl.BlockSpec(memory_space=pltpu.SMEM)

time: 150 us -> 153 us (1.020)
  Pallas kernels: 149 us -> 151 us
    pallas_call x1, Pallas kernels: 143 us -> 145 us  [body(): pl.pallas_call(lambda *refs: kernel(n, types.SimpleNamespace(**dict(zip(n...]
where the time goes in v2:
time: 153 us
  Pallas kernels  151 us (99%)
    pallas_call x1, Pallas kernels, body(): pl.pallas_call(lambda *refs: kernel(n, types.SimpleNamespace(**dict(zip(n...  145 us
    pallas_call x1, Pallas kernels, finish(): pl.pallas_call(spread, grid=(steps,), out_shape=[shape(output.shape, low)...  5.84 us

profile of v2, /device:TPU:0, one launch (start us, length us, event | category | flops | bytes accessed | tf_op | source)
XLA Modules:
  0.0 152.7 jit_solution(448728545592712355)
XLA Ops:
  1.3 145.3 %shard_map.254 = (bf16[298,768]{1,0:T(8,128)(2,1)}, f32[298,768]{1,0:T(8,128)}, f32[8,768]{1,0:T(8,128)}, bf16[1536,768]{1,0:T(8,128)(2,1)}, bf16[768,768]{1,0:T(8,128)(2,1)}) custom-call(bf16[298,768]{1,0:T(8,128)(2,1)} %refs_0_.1, s32[1]{0:T(128)S(6)} %copy.29.refs_1_, f32[768]{0:T(1024)} %refs_2_.1, f32[768]{0:T(1024)} %refs_3_.1, f32[2,192]{1,0:T(2,128)} %refs_4_.1, ...), custom_call_target="tpu_custom_call" | custom-call | tf_op jit(solution)/shard_map/pallas_call | solution.py:1084
  146.6 5.8 %shard_map.255 = (bf16[298,768]{1,0:T(8,128)(2,1)}, f32[298,768]{1,0:T(8,128)}, f32[768,768]{1,0:T(8,128)}, f32[768,768]{1,0:T(8,128)}, f32[3,192,768]{2,1,0:T(8...) custom-call(bf16[298,768]{1,0:T(8,128)(2,1)} %get-tuple-element.33.o, ...), custom_call_target="tpu_custom_call" | custom-call | tf_op jit(solution)/shard_map/pallas_call | solution.py:994

commit v3 on v0

--- a/solution.py
+++ b/solution.py
@@ -437,21 +437,21 @@
 
 PLAN = dict(
     waiting=(),
-    shared=(0, 1),
-    arriving=(),
-    h0p0=(2, 0),
-    h0p2=(2, 3, 0, 1),
-    h0=(),
-    h1p0=(3, 0),
-    h1p2=(1,),
-    h1=(3,),
-    h2p0=(2, 0, 4),
-    h2p2=(3, 1, 5, 6, 2),
-    h2=(3, 4),
-    led=(2, 5),
-    crossing=(7, 3, 4, 6),
-    told=(5, 7, 0),
-    end=(2, 1, 6, 4, 5, 7, 6, 7, 1),
+    shared=(0,),
+    arriving=(0,),
+    h0p0=(2,),
+    h0p2=(2, 1, 3, 0),
+    h0=(1,),
+    h1p0=(0, 3),
+    h1p2=(1, 0),
+    h1=(3, 2, 4),
+    h2p0=(0, 1, 3),
+    h2p2=(5, 2, 6, 3),
+    h2=(4,),
+    led=(7, 2, 3, 5, 6, 4),
+    crossing=(7, 1, 2),
+    told=(5, 4),
+    end=(6, 5, 7, 6, 1, 7),
 )
 
 

time: 150 us -> 153 us (1.020)
  Pallas kernels: 149 us -> 151 us
    pallas_call x1, Pallas kernels: 143 us -> 146 us  [body(): pl.pallas_call(lambda *refs: kernel(n, types.SimpleNamespace(**dict(zip(n...]
where the time goes in v3:
time: 153 us
  Pallas kernels  151 us (99%)
    pallas_call x1, Pallas kernels, body(): pl.pallas_call(lambda *refs: kernel(n, types.SimpleNamespace(**dict(zip(n...  146 us
    pallas_call x1, Pallas kernels, finish(): pl.pallas_call(spread, grid=(steps,), out_shape=[shape(output.shape, low)...  5.82 us

profile of v3, /device:TPU:0, one launch (start us, length us, event | category | flops | bytes accessed | tf_op | source)
XLA Modules:
  0.0 152.8 jit_solution(16671026175304286124)
XLA Ops:
  1.3 145.5 %shard_map.254 = (bf16[298,768]{1,0:T(8,128)(2,1)}, f32[298,768]{1,0:T(8,128)}, f32[8,768]{1,0:T(8,128)}, bf16[1536,768]{1,0:T(8,128)(2,1)}, bf16[768,768]{1,0:T(8,128)(2,1)}) custom-call(bf16[298,768]{1,0:T(8,128)(2,1)} %refs_0_.1, s32[1]{0:T(128)S(6)} %copy.29.refs_1_, f32[768]{0:T(1024)} %refs_2_.1, f32[768]{0:T(1024)} %refs_3_.1, f32[2,192]{1,0:T(2,128)} %refs_4_.1, ...), custom_call_target="tpu_custom_call" | custom-call | tf_op jit(solution)/shard_map/pallas_call | solution.py:1078
  146.8 5.8 %shard_map.255 = (bf16[298,768]{1,0:T(8,128)(2,1)}, f32[298,768]{1,0:T(8,128)}, f32[768,768]{1,0:T(8,128)}, f32[768,768]{1,0:T(8,128)}, f32[3,192,768]{2,1,0:T(8...) custom-call(bf16[298,768]{1,0:T(8,128)(2,1)} %get-tuple-element.33.o, ...), custom_call_target="tpu_custom_call" | custom-call | tf_op jit(solution)/shard_map/pallas_call | solution.py:989
